TPU v7x, 256 devices: a whole 4x4x8 slice. The times are simulated.
256 devices in a mesh: leaf: 4 (over y), col: 64 (over x, z, core).
Axes of the slice: x: 4, y: 4, z: 8, core: 2. Of those that a mesh axis runs over, the one named last changes fastest.
Arguments:
- node_rhs: float32 [4, 64, 9, 256, 256], P('leaf', 'col'), may hold values from -0.125 to 0.125
- node_inverse: float32 [4, 64, 9, 256, 256], P('leaf', 'col')
- local_blocks: float32 [4, 64, 8, 2, 64, 256], P('leaf', 'col'), may hold values from -0.09375 to 0.09375
- chain_next: float32 [4, 64, 256, 256], P('leaf', 'col')
- chain_top: float32 [4, 64, 64, 256], P('leaf', 'col'), may hold values from -0.09375 to 0.09375
- top_rhs: float32 [4, 256, 256], replicated, may hold values from -6 to 6
- top_inverse: float32 [4, 256, 256], replicated
- top_next: float32 [3, 256, 256], replicated, may hold values from -0.1875 to 0.1875
- ancestors: int32 [4, 64, 8, 2], P('leaf', 'col'), may hold values from 0 to 8, as said below
- block_rows: int32 [4, 64, 8, 2, 64], P('leaf', 'col'), may hold values from 0 to 255, as said below
- chain_target: int32 [4, 64], P('leaf', 'col'), may hold values from 0 to 3
- chain_rows: int32 [4, 64, 64], P('leaf', 'col'), may hold values from 0 to 255, as said below
Outputs:
- node_solution: float32 [4, 64, 9, 256, 256], P('leaf', 'col')
- top_solution: float32 [4, 256, 256], replicated
Inputs may be any that keep to these rules, and one draw needn't show every extreme that they name: `ancestors`: entry 0 of supernode k's list is its parent, between k + 1 and 8 (8 names the device's separator supernode); entry 1 is a top supernode, 0 to 3. `block_rows`: distinct and increasing within each block. `chain_rows`: distinct and increasing within each block.
All inputs are finite; a program needn't handle non-finite values.
Results may differ from a plain program's by a relative error of at most 0.0003.
Values sent between devices are 32-bit elements; how exact they have to be, the bound alone decides.
A program may use at most 192 MiB of HBM per device.

v0:
```python
import jax
import jax.numpy as jnp
from jax import lax
from jax.sharding import PartitionSpec as P

precise = lax.Precision.HIGHEST


def prefix(value, axis, join, neutral, backward):
    count, mine = (lax.axis_size(axis), lax.axis_index(axis))
    pieces = jax.tree.map(lambda part: lax.all_gather(part, axis), value)
    if backward:
        pieces = jax.tree.map(lambda part: part[::-1], pieces)
        mine = count - 1 - mine
    subtotal = jax.tree.map(
        lambda part, zero: jnp.full_like(part, 0) + jnp.asarray(zero, part.dtype), value, neutral
    )

    def hop(position, subtotal):
        longer = join(subtotal, jax.tree.map(lambda part: part[position], pieces))
        return jax.tree.map(lambda new, old: jnp.where(position < mine, new, old), longer, subtotal)

    return lax.fori_loop(0, count - 1, hop, subtotal)


def product(left, right):
    return jnp.dot(left, right, precision=precise, preferred_element_type=jnp.float32)


def transposed(left, right):
    return lax.dot_general(
        left, right, (((0,), (0,)), ((), ())), precision=precise, preferred_element_type=jnp.float32
    )


def compose(earlier, later):
    return (product(later[0], earlier[0]), product(later[0], earlier[1]) + later[1])


def local_forward(source, inverse, blocks, links, row_index, top_count):
    node_count = source.shape[0]
    local_count = node_count - 1
    pending = jnp.zeros(source.shape, jnp.float32)
    upward = jnp.zeros((top_count,) + source.shape[1:], jnp.float32)
    solved = []
    for member in range(local_count):
        result = product(inverse[member], source[member] - pending[member])
        solved.append(result)
        pending = pending.at[links[member, 0], row_index[member, 0]].add(
            product(blocks[member, 0], result)
        )
        upward = upward.at[links[member, 1], row_index[member, 1]].add(
            product(blocks[member, 1], result)
        )
    return (jnp.stack(solved), source[local_count] - pending[local_count], upward)


def local_backward(solved, chain_value, inverse, blocks, links, row_index, top_values):
    local_count = solved.shape[0]
    known_values = jnp.concatenate([jnp.zeros_like(solved), chain_value[None]], axis=0)
    for member in reversed(range(local_count)):
        above_rows = known_values[links[member, 0], row_index[member, 0]]
        beyond = top_values[links[member, 1], row_index[member, 1]]
        result = (
            solved[member]
            - transposed(blocks[member, 0], above_rows)
            - transposed(blocks[member, 1], beyond)
        )
        known_values = known_values.at[member].set(transposed(inverse[member], result))
    return known_values


def top_solve(source, inverse, coupling):
    top_count = source.shape[0]
    forward = []
    for member in range(top_count):
        result = source[member]
        if member > 0:
            result = result - product(coupling[member - 1], forward[-1])
        forward.append(product(inverse[member], result))
    backward = [None] * top_count
    for member in reversed(range(top_count)):
        result = forward[member]
        if member < top_count - 1:
            result = result - transposed(coupling[member], backward[member + 1])
        backward[member] = transposed(inverse[member], result)
    return jnp.stack(backward)


def shards(
    node_rhs,
    node_inverse,
    local_blocks,
    chain_next,
    chain_top,
    top_rhs,
    top_inverse,
    top_next,
    ancestors,
    block_rows,
    chain_target,
    chain_rows,
):
    source = node_rhs[0, 0]
    inverse = node_inverse[0, 0]
    blocks = local_blocks[0, 0]
    links = ancestors[0, 0]
    row_index = block_rows[0, 0]
    sideways = chain_top[0, 0]
    target = chain_target[0, 0]
    row_here = chain_rows[0, 0]
    columns = lax.axis_size("col")
    position = lax.axis_index("col")
    onward = jnp.where(position == columns - 1, jnp.zeros_like(chain_next[0, 0]), chain_next[0, 0])
    solved, residual, upward = local_forward(
        source, inverse, blocks, links, row_index, top_rhs.shape[0]
    )
    chain_inverse = inverse[-1]
    extent = residual.shape[0]
    identity = (jnp.eye(extent, dtype=jnp.float32), jnp.zeros_like(residual))
    step_map = -product(onward, chain_inverse)
    step_shift = product(onward, product(chain_inverse, residual))
    incoming = prefix((step_map, step_shift), "col", compose, identity, False)[1]
    chain_value = product(chain_inverse, residual - incoming)
    upward = upward.at[target, row_here].add(product(sideways, chain_value))
    summed = lax.psum(upward, ("leaf", "col"))
    top_values = top_solve(top_rhs - summed, top_inverse, top_next)
    lowered = chain_value - transposed(sideways, top_values[target, row_here])
    back_map = -lax.dot_general(
        chain_inverse,
        onward,
        (((0,), (1,)), ((), ())),
        precision=precise,
        preferred_element_type=jnp.float32,
    )
    back_shift = transposed(chain_inverse, lowered)
    above_value = prefix((back_map, back_shift), "col", compose, identity, True)[1]
    chain_solution = product(back_map, above_value) + back_shift
    node_solution = local_backward(
        solved, chain_solution, inverse, blocks, links, row_index, top_values
    )
    return (node_solution[None, None], top_values)


def solution(mesh):
    placed = (
        P("leaf", "col", None, None, None),
        P("leaf", "col", None, None, None),
        P("leaf", "col", None, None, None, None),
        P("leaf", "col", None, None),
        P("leaf", "col", None, None),
        P(),
        P(),
        P(),
        P("leaf", "col", None, None),
        P("leaf", "col", None, None, None),
        P("leaf", "col"),
        P("leaf", "col", None),
    )
    return jax.shard_map(
        shards,
        mesh=mesh,
        in_specs=placed,
        out_specs=(P("leaf", "col", None, None, None), P()),
        check_vma=False,
    )
```

profile of v0, /device:TPU:1, one launch (start us, length us, event | category | flops | bytes accessed | tf_op | source)
XLA Modules:
  0.0 1161.0 jit_solution(10315489652709513804)
XLA Ops:
  30.9 5.1 scatter_fusion
  38.7 5.1 scatter_fusion.1
  46.5 5.1 scatter_fusion.2
  54.3 5.1 scatter_fusion.3
  62.1 5.1 scatter_fusion.4
  77.6 5.1 scatter_fusion.6
  85.4 5.3 scatter_fusion.7
  126.9 5.1 scatter_fusion.10
  133.9 5.1 scatter_fusion.11
  141.0 5.1 scatter_fusion.12
  148.1 5.1 scatter_fusion.13
  155.2 5.1 scatter_fusion.14
  162.3 5.1 scatter_fusion.15
  167.4 31.8 %all-gather.13.cloned.1.call-done = f32[16384,256]{1,0:T(8,128)} async-done(((f32[256,256]{1,0:T(8,128)}), f32[16384,256]{1,0:T(8,128)}) %all-gather.13.cloned.1.call-update) | async-done | bytes 16777232 | tf_op jit(solution)/shard_map/all_gather | solution.py:11
  199.2 100.1 %all-gather.11.cloned.1.call-done = f32[16384,256]{1,0:T(8,128)} async-done(((f32[256,256]{1,0:T(8,128)}), f32[16384,256]{1,0:T(8,128)}) %all-gather.11.cloned.1.call-update) | async-done | bytes 16777232 | tf_op jit(solution)/shard_map/all_gather | solution.py:11
  299.3 194.1 %while.36 = (s32[]{:T(128)}, f32[256,256]{1,0:T(8,128)}, s32[]{:T(128)}, f32[64,256,256]{2,1,0:T(8,128)}, f32[64,256,256]{2,1,0:T(8,128)}, /*index=5*/s32[]{:T(128)}, s32[]{:T(128)}) while((s32[]{:T(128)}, f32[256,256]{1,0:T(8,128)}, s32[]{:T(128)}, f32[64,256,256]{2,1,0:T(8,128)}, f32[64,256,256]{2,1,0:T(8,128)}, ...), condition=%wide.region_9.10_spmd.clone, body=%wide.region_8.9_spmd.clone.sunk | while | flops 201588736 | bytes 1837663 | solution.py:23
  501.6 250.6 %all-reduce.20.cloned.1.call-done = f32[4,256,256]{2,1,0:T(8,128)} async-done(((f32[4,256,256]{2,1,0:T(8,128)}), f32[4,256,256]{2,1,0:T(8,128)}) %all-reduce.20.cloned.1.call-update) | async-done | bytes 1048592 | tf_op jit(solution)/shard_map/psum | solution.py:126
  764.1 99.0 %all-gather.9.cloned.1.call-done = f32[16384,256]{0,1:T(8,128)} async-done(((f32[256,256]{0,1:T(8,128)}), f32[16384,256]{0,1:T(8,128)}) %all-gather.9.cloned.1.call-update) | async-done | bytes 16777232 | tf_op jit(solution)/shard_map/all_gather | solution.py:11
  863.1 17.9 %copy.37 = f32[16384,256]{1,0:T(8,128)} copy(f32[16384,256]{0,1:T(8,128)} %all-gather.9.cloned.1.call-done) | data formatting | bytes 33554432 | tf_op jit(solution)/shard_map/all_gather | solution.py:11
  881.0 11.5 rev.6
  904.7 65.5 %all-gather.15.cloned.1.call-done = f32[16384,256]{0,1:T(8,128)} async-done(((f32[256,256]{0,1:T(8,128)}), f32[16384,256]{0,1:T(8,128)}) %all-gather.15.cloned.1.call-update) | async-done | bytes 16777232 | tf_op jit(solution)/shard_map/all_gather | solution.py:11
  970.2 17.4 %copy.38 = f32[16384,256]{1,0:T(8,128)} copy(f32[16384,256]{0,1:T(8,128)} %all-gather.15.cloned.1.call-done) | data formatting | bytes 33554432 | tf_op jit(solution)/shard_map/all_gather | solution.py:11
  987.6 11.4 rev.7
  999.1 94.1 %while.37 = (s32[]{:T(128)}, f32[256,256]{1,0:T(8,128)S(1)}, s32[]{:T(128)}, f32[64,256,256]{2,1,0:T(8,128)}, f32[64,256,256]{2,1,0:T(8,128)}, /*index=5*/s32[]{:T(128)}, s32[]{:T(128)}) while((s32[]{:T(128)}, f32[256,256]{1,0:T(8,128)S(1)}, s32[]{:T(128)}, f32[64,256,256]{2,1,0:T(8,128)}, f32[64,256,256]{2,1,0:T(8,128)}, ...), condition=%wide.region_21.22_spmd.clone, body=%wide.region_20.21_spmd.clone.sunk | while | flops 201588736 | bytes 1837663 | solution.py:23
  (434 shorter events, 440.8 us)
Async XLA Ops:
  7.2 487.9 %copy-start = (f32[1,1,64,256]{3,2,1,0:T(8,128)S(1)}, f32[1,1,64,256]{3,2,1,0:T(8,128)}, u32[]{:S(2)}) copy-start(f32[1,1,64,256]{3,2,1,0:T(8,128)} %param.36) | copy-start | bytes 196612
  7.2 192.0 %all-gather.13.cloned.1.call-start = ((), (), s32[]{:S(2)}) async-start(), calls=%async_computation.3 | async-start | bytes 17039360 | tf_op jit(solution)/shard_map/all_gather | solution.py:11
  28.1 2.6 copy-start.7
  30.7 7.0 copy-start.5
  43.8 10.4 copy-start.28
  95.2 204.1 %all-gather.11.cloned.1.call-start = ((), (), s32[]{:S(2)}) async-start(), calls=%async_computation.2 | async-start | bytes 17039360 | tf_op jit(solution)/shard_map/all_gather | solution.py:11
  97.4 654.8 %all-reduce.20.cloned.1.call-start = ((), (), s32[]{:S(2)}) async-start(), calls=%async_computation | async-start | bytes 2097152 | tf_op jit(solution)/shard_map/psum | solution.py:126
  499.7 254.1 %copy-start.4 = (f32[4,256,256]{2,1,0:T(8,128)S(1)}, f32[4,256,256]{2,1,0:T(8,128)}, u32[]{:S(2)}) copy-start(f32[4,256,256]{2,1,0:T(8,128)} %param.38) | copy-start | bytes 3145732
  500.7 253.7 %copy-start.16 = (f32[3,256,256]{2,1,0:T(8,128)S(1)}, f32[3,256,256]{2,1,0:T(8,128)}, u32[]{:S(2)}) copy-start(f32[3,256,256]{2,1,0:T(8,128)} %param.39) | copy-start | bytes 2359300
  500.7 362.4 %all-gather.9.cloned.1.call-start = ((), (), s32[]{:S(2)}) async-start(), calls=%async_computation.1 | async-start | bytes 17039360 | tf_op jit(solution)/shard_map/all_gather | solution.py:11
  501.3 468.9 %all-gather.15.cloned.1.call-start = ((), (), s32[]{:S(2)}) async-start(), calls=%async_computation.4 | async-start | bytes 17039360 | tf_op jit(solution)/shard_map/all_gather | solution.py:11
  760.6 142.5 %copy-start.3 = (f32[4,256,256]{2,1,0:T(8,128)}, f32[4,256,256]{2,1,0:T(8,128)S(1)}, u32[]{:S(2)}) copy-start(f32[4,256,256]{2,1,0:T(8,128)S(1)} %copy.15) | copy-start | bytes 3145732
  999.1 94.1 %copy-start.15 = (f32[256,256]{1,0:T(8,128)S(1)}, f32[256,256]{1,0:T(8,128)}, u32[]{:S(2)}) copy-start(f32[256,256]{1,0:T(8,128)} %convolution_negate_fusion) | copy-start | bytes 786436
  999.1 94.1 %copy-start.19 = (f32[256,256]{0,1:T(8,128)S(1)}, f32[256,256]{0,1:T(8,128)}, u32[]{:S(2)}) copy-start(f32[256,256]{0,1:T(8,128)} %convolution_bitcast_fusion.8) | copy-start | bytes 786436
  1094.0 4.2 copy-start.6
  1094.0 5.6 copy-start.27
  1101.4 5.6 copy-start.26
  1108.8 5.6 copy-start.25
  1116.2 5.8 copy-start.24
  1123.8 5.6 copy-start.23
  1131.2 5.6 copy-start.22
  1138.6 5.0 copy-start.21
  1145.3 5.0 copy-start.20
  1150.8 3.6 copy-start.1
  (10 other events, 10.2 us)
Sparse Core Ops, SparseCore 0:
  95.3 103.8 all-gather.12
  202.6 96.6 all-gather.10
  500.8 251.2 all-reduce.19
  755.5 107.6 all-gather.8
  865.9 104.2 all-gather.14
where the time goes:
time: 1180 us; the launch traced here: 1160 us
  waiting for transfers between devices  548 us (46%)
  matrix products  305 us (26%)
  local copies, waits for them, and re-layouts  171 us (14%)
  other arithmetic  88.5 us (8%)
  between operations  45.8 us (4%)
    all_gather x4, waiting for transfers between devices, prefix(): pieces = jax.tree.map(lambda part: lax.all_gather(part, axis), value)  296 us
    dot_general x162, matrix products, product(): jnp.dot(left, right, precision=precise, preferred_element_type=jnp.float32)  273 us
    psum x1, waiting for transfers between devices, shards(): summed = lax.psum(upward, ('leaf', 'col'))  251 us
    while x126, local copies, waits for them, and re-layouts  61 us
    scatter-add x8, other arithmetic, local_forward(): pending.at[links[member, 0], row_index[member, 0]]  41.1 us
    scatter-add x8, other arithmetic, local_forward(): upward.at[links[member, 1], row_index[member, 1]]  40.9 us
    all_gather x2, local copies, waits for them, and re-layouts, prefix(): pieces = jax.tree.map(lambda part: lax.all_gather(part, axis), value)  35.3 us
    dot_general x33, matrix products, transposed(): lax.dot_general(left, right, (((0,), (0,)), ((), ())), precision=precise,...  30.5 us
  transfers between devices with their start and end apart: 5, of which 5 were waited for; matrix products, arithmetic and copies ran while one was open for 10% of the time, Pallas kernels for 0%

commit v1 on v0

v1 whole, which is shorter than its diff:
```python
import jax
import jax.numpy as jnp
from jax import lax
from jax.experimental import pallas as pl
from jax.experimental.pallas import tpu as pltpu
from jax.sharding import PartitionSpec as P

F32 = jnp.float32
BF16 = jnp.bfloat16
MESH = pl.DeviceIdType.MESH
NX, NZ, NY, NCOL = 4, 8, 4, 64
W = 256
H = 128
Q = 16
LOC = 8
TOP = 4


def split(value):
    if isinstance(value, tuple):
        return value
    high = value.astype(BF16)
    return high, (value - high.astype(F32)).astype(BF16)


def once(left, right, dims):
    return lax.dot_general(left, right, (dims, ((), ())), preferred_element_type=F32)


def thrice(left, right, dims):
    lh, ll = split(left)
    rh, rl = split(right)
    return once(lh, rh, dims) + (once(lh, rl, dims) + once(ll, rh, dims))


def nn(left, right):
    return thrice(left, right, ((1,), (0,)))


def nt(left, right):
    return thrice(left, right, ((1,), (1,)))


def tn(left, right):
    return thrice(left, right, ((0,), (0,)))


def one_hot(index_row, extent):
    place = lax.broadcasted_iota(jnp.int32, (extent, index_row.shape[1]), 0)
    return jnp.where(place == index_row, 1.0, 0.0).astype(BF16)


def kernel(
    links, target, rhs, inverse, blocks, onward, sideways, top_rhs, top_inverse, top_next, rows, chain_rows,
    out, top_out,
    src, dh, dl, ddh, ddl, hval, upn, upt, uprecv, uph, ybuf, uy, zred,
    a_own, a_sib, a0, a1, msel, nfull, acf, ach, acl, fh, fl, gh, gl, vbuf, pall,
    rt, ex_s, ex_r, schip, sbuf, z0, zsend, zbuf, zback, xin_f, xout_f,
    ar_a, ar_b, ar_c, ar_d, topx, topt, trt, tih, til, kh, kl, lh, ll,
    bt, m_s, m_r, bchip, bbuf, xsend, xback, xin_b, xout_b, mb_s, mb_r,
    core_s, core_r, ac_s, ac_r, acx_s, acx_r, v_s, v_r, vx_s, vx_r, vo_s, vo_r,
    s_s, s_r, up_s, up_r, y_s, y_r, zr_s, zr_r, xf_s, xf_r, zb_s, zb_r, ar_s, ar_r,
    b_s, b_r, xb_s, xb_r, xa_s, xa_r, tp_s, tp_r,
):
    leaf = lax.axis_index("leaf")
    col = lax.axis_index("col")
    x, z, q = col // 16, (col // 2) % NZ, col % 2

    def at(xx, zz, qq):
        return (leaf, xx * 16 + zz * 2 + qq)

    sibling = at(x, z, 1 - q)

    def zpeer(d):
        return at(x, lax.rem(z + d, NZ), q)

    def xpeer(d):
        return at(lax.rem(x + d, NX), z, q)

    def ypeer(d):
        return (lax.rem(leaf + d, NY), col)

    def zfrom(d):
        return lax.rem(z + NZ - d, NZ)

    def xfrom(d):
        return lax.rem(x + NX - d, NX)

    def yfrom(d):
        return lax.rem(leaf + NY - d, NY)

    def copy(source, goal, ss, rs, device):
        return pltpu.make_async_remote_copy(
            src_ref=source, dst_ref=goal, send_sem=ss, recv_sem=rs, device_id=device, device_id_type=MESH
        )

    def swap(source, goal, number):
        return copy(source, goal, core_s.at[number], core_r.at[number], sibling)

    barrier = pltpu.get_barrier_semaphore()
    peers = [sibling] + [zpeer(d) for d in range(1, NZ)] + [xpeer(d) for d in range(1, NX)]
    peers = peers + [ypeer(d) for d in range(1, NY)]
    for peer in peers:
        pl.semaphore_signal(barrier, inc=1, device_id=peer, device_id_type=MESH)

    first = q == 0
    half = pl.ds(pl.multiple_of(q * H, H), H)
    other = pl.ds(pl.multiple_of((1 - q) * H, H), H)

    def rows_of(zz):
        return pl.ds(pl.multiple_of(zz * Q, Q), Q)

    chain_inverse = split(inverse[LOC])
    coupling = jnp.where(col == NCOL - 1, jnp.zeros((W, W), F32), onward[...])
    a_own[...] = -nn(coupling, chain_inverse)
    side = nn(sideways[...], chain_inverse)
    side_h, side_l = split(side)
    spread = one_hot(chain_rows[...], W)
    nfull[...] = once(spread, side_h, ((1,), (0,))) + once(spread, side_l, ((1,), (0,)))

    pl.semaphore_wait(barrier, len(peers))
    swap_a = swap(a_own, a_sib, 0)
    swap_a.start()

    def local_map(k, carry):
        near = nn(blocks[k], inverse[k])
        near_h, near_l = split(near)
        to_parent = one_hot(rows[pl.ds(2 * k, 1), :], W)
        to_top = one_hot(rows[pl.ds(2 * k + 1, 1), :], W)
        dh[k] = once(to_parent, near_h[:64], ((1,), (0,))).astype(BF16)
        dl[k] = once(to_parent, near_l[:64], ((1,), (0,))).astype(BF16)
        ddh[k] = once(to_top, near_h[64:], ((1,), (0,))).astype(BF16)
        ddl[k] = once(to_top, near_l[64:], ((1,), (0,))).astype(BF16)
        return carry

    lax.fori_loop(0, LOC, local_map, 0)

    swap_a.wait()
    a0[...] = jnp.where(first, a_own[...], a_sib[...])
    a1[...] = jnp.where(first, a_sib[...], a_own[...])
    pair = nn(a1[...], a0[...])
    msel[...] = jnp.where(first, pair, a_own[...])
    acf[z] = pair.T
    vbuf[z, q, pl.ds(0, 64)] = jnp.where(first, side, nn(side, a0[...]))
    index = (chain_rows[...] + target[0] * W).astype(F32)
    empty = jnp.zeros((1, 64), F32)
    index = jnp.concatenate(
        [jnp.where(first, index, empty), jnp.where(first, empty, index), jnp.zeros((1, 128), F32)], axis=1
    )
    vbuf[z, q, pl.ds(64, 8)] = jnp.broadcast_to(index, (8, W))

    def ac_copy(d):
        return copy(acf.at[z, half], acf.at[z, half], ac_s.at[d], ac_r.at[d], zpeer(d))

    def v_copy(d):
        return copy(vbuf.at[z, q], vbuf.at[z, q], v_s.at[d], v_r.at[d], zpeer(d))

    order = (1, 7, 2, 6, 3, 5, 4)
    for d in order:
        ac_copy(d).start()
    v_own = copy(vbuf.at[z, q], vbuf.at[z, q], vo_s.at[0], vo_r.at[0], sibling)
    v_own.start()
    for d in order:
        v_copy(d).start()

    for k in range(LOC + 1):
        src[k] = rhs[k]
    for k in range(LOC):
        update = nn((dh[k], dl[k]), src[k])
        for j in range(k + 1, LOC + 1):
            src[j] = src[j] - jnp.where(links[k, 0] == j, update, 0.0)

    rt[...] = src[LOC].T
    ex_s[...] = jnp.where(first, -nt(rt[...], a_own[...]), rt[...])
    swap_s = swap(ex_s, ex_r, 1)
    swap_s.start()
    swap_s.wait()
    shift_half = jnp.where(first, ex_s[half], ex_r[half])
    rest_half = jnp.where(first, ex_r[half], ex_s[half])
    schip[...] = -nt(rest_half - shift_half, a1[...])

    def s_copy(d):
        to = lax.rem(z + d, NZ)
        return copy(schip.at[rows_of(to)], sbuf.at[z], s_s.at[d], s_r.at[d], zpeer(d))

    for d in order:
        s_copy(d).start()
    sbuf[z] = schip[rows_of(z)]

    for t in range(TOP):
        upn[t] = jnp.zeros((W, W), F32)

    def local_up(k, carry):
        part = nn((ddh[k], ddl[k]), src[k])
        for t in range(TOP):
            upn[t] = upn[t] + jnp.where(links[k, 1] == t, part, 0.0)
        return carry

    lax.fori_loop(0, LOC, local_up, 0)
    chain_part = nt(jnp.where(first, rt[...], rt[...] - ex_r[...]), nfull[...])
    for t in range(TOP):
        upt[t] = upn[t].T + jnp.where(target[0] == t, chain_part, 0.0)
    swap_u = copy(upt.at[:, other], uprecv, up_s.at[0], up_r.at[0], sibling)
    swap_u.start()

    def square(k, carry):
        here = split(inverse[k])
        hval[k] = tn(here, nn(here, src[k]))
        return carry

    lax.fori_loop(0, LOC // 2, square, 0)
    swap_u.wait()
    for t in range(TOP):
        uph[t] = upt[t, half] + uprecv[t]

    def y_copy(d):
        return copy(uph.at[lax.rem(leaf + d, NY)], ybuf.at[leaf], y_s.at[d], y_r.at[d], ypeer(d))

    for d in range(1, NY):
        y_copy(d).start()
    ybuf[leaf] = uph[leaf]
    lax.fori_loop(LOC // 2, LOC, square, 0)

    for t in range(TOP):
        th, tl = split(top_inverse[t])
        tih[t] = th
        til[t] = tl
        trt[t] = top_rhs[t].T
    for t in range(TOP - 1):
        kh[t], kl[t] = split(nn((tih[t + 1], til[t + 1]), top_next[t]))
        lh[t], ll[t] = split(nn(top_next[t], (tih[t], til[t])))

    def ac_pass(d):
        part = acf.at[zfrom(d), half]
        return copy(part, part, acx_s.at[d], acx_r.at[d], sibling)

    def ac_come(d):
        part = acf.at[zfrom(d), half]
        return copy(part, part, ac_s.at[d], ac_r.at[d], zpeer(d))

    def ac_passed(d):
        part = acf.at[zfrom(d), other]
        return copy(part, part, acx_s.at[d], acx_r.at[d], sibling)

    def v_come(d):
        part = vbuf.at[zfrom(d), q]
        return copy(part, part, v_s.at[d], v_r.at[d], zpeer(d))

    def v_pass(d):
        part = vbuf.at[zfrom(d), q]
        return copy(part, part, vx_s.at[d], vx_r.at[d], sibling)

    def v_passed(d):
        part = vbuf.at[zfrom(d), 1 - q]
        return copy(part, part, vx_s.at[d], vx_r.at[d], sibling)

    for d in order:
        ac_come(d).wait_recv()
        ac_pass(d).start()
    for d in range(1, NY):
        copy(uph.at[0], ybuf.at[yfrom(d)], y_s.at[d], y_r.at[d], ypeer(d)).wait_recv()
    uy[...] = (ybuf[0] + ybuf[1]) + (ybuf[2] + ybuf[3])

    def zr_copy(d):
        to = lax.rem(z + d, NZ)
        return copy(uy.at[rows_of(to)], zred.at[z], zr_s.at[d], zr_r.at[d], zpeer(d))

    for d in order:
        zr_copy(d).start()
    zred[z] = uy[rows_of(z)]
    for d in order:
        ac_passed(d).wait_recv()

    def halves(c, carry):
        ach[c], acl[c] = split(acf[c])
        return carry

    lax.fori_loop(0, NZ, halves, 0)
    for d in order:
        copy(schip.at[pl.ds(0, Q)], sbuf.at[zfrom(d)], s_s.at[d], s_r.at[d], zpeer(d)).wait_recv()

    z0[0] = sbuf[0]
    fh[0] = ach[0]
    fl[0] = acl[0]

    def prefix(c, carry):
        here = (ach[c], acl[c])
        z0[c] = sbuf[c] + nn(z0[c - 1], here)
        fh[c], fl[c] = split(nn((fh[c - 1], fl[c - 1]), here))
        return carry

    lax.fori_loop(1, NZ, prefix, 0)

    whole = (fh[NZ - 1], fl[NZ - 1])
    hop_f = copy(xout_f, xin_f, xf_s.at[0], xf_r.at[0], at(lax.rem(x + 1, NX), z, q))

    @pl.when(x == 0)
    def _():
        xin_f[...] = jnp.zeros((Q, W), F32)
        xout_f[...] = z0[NZ - 1]

    @pl.when(x > 0)
    def _():
        hop_f.wait_recv()
        xout_f[...] = z0[NZ - 1] + nn(xin_f[...], whole)

    @pl.when(x < NX - 1)
    def _():
        hop_f.start()

    entering = split(xin_f[...])
    zsend[0] = xin_f[...]

    def fix(c, carry):
        zsend[c] = z0[c - 1] + nn(entering, (fh[c - 1], fl[c - 1]))
        return carry

    lax.fori_loop(1, NZ, fix, 0)

    def zb_copy(d):
        to = lax.rem(z + d, NZ)
        return copy(zsend.at[to], zback.at[rows_of(z)], zb_s.at[d], zb_r.at[d], zpeer(d))

    for d in order:
        zb_copy(d).start()
    zback[rows_of(z)] = zsend[z]

    for d in order:
        v_come(d).wait_recv()
        v_pass(d).start()
    v_own_come = copy(vbuf.at[z, 1 - q], vbuf.at[z, 1 - q], vo_s.at[0], vo_r.at[0], sibling)
    v_own_come.wait_recv()
    for d in order:
        v_passed(d).wait_recv()

    flows = []
    for c in range(NZ):
        found = (vbuf[c, 0, pl.ds(64, 1), pl.ds(0, H)] + vbuf[c, 1, pl.ds(64, 1), pl.ds(0, H)]).astype(jnp.int32)
        pall[:, c * H : (c + 1) * H] = one_hot(found, TOP * W)
        reach = jnp.concatenate([vbuf[c, 0, pl.ds(0, 64)], vbuf[c, 1, pl.ds(0, 64)]], axis=0)
        flows.append(nt(zsend[c], reach))
    flow_h, flow_l = split(jnp.concatenate(flows, axis=1))
    for d in order:
        copy(uy.at[pl.ds(0, Q)], zred.at[zfrom(d)], zr_s.at[d], zr_r.at[d], zpeer(d)).wait_recv()
    reduced = zred[0]
    for c in range(1, NZ):
        reduced = reduced + zred[c]
    for t in range(TOP):
        places = pall[t * W : (t + 1) * W, :]
        down = once(flow_h, places, ((1,), (1,))) + once(flow_l, places, ((1,), (1,)))
        part = jnp.where(leaf == t, reduced, 0.0) - down
        if t < 2:
            ar_a[x, t] = part
        else:
            ar_b[leaf, t - 2] = part

    def ar_copy(buf, mine, number, device):
        return copy(buf.at[mine], buf.at[mine], ar_s.at[number], ar_r.at[number], device)

    for d in range(1, NX):
        ar_copy(ar_a, x, d, xpeer(d)).start()
        ar_copy(ar_b, leaf, 4 + d, ypeer(d)).start()

    gh[NZ - 1] = ach[NZ - 1]
    gl[NZ - 1] = acl[NZ - 1]

    def suffix(i, carry):
        c = NZ - 1 - i
        gh[c], gl[c] = split(nn((ach[c], acl[c]), (gh[c + 1], gl[c + 1])))
        return carry

    lax.fori_loop(1, NZ, suffix, 0)

    for d in order:
        copy(zsend.at[0], zback.at[rows_of(zfrom(d))], zb_s.at[d], zb_r.at[d], zpeer(d)).wait_recv()
    swap_z = swap(zback, zbuf, 2)
    swap_z.start()

    for d in range(1, NX):
        ar_copy(ar_a, xfrom(d), d, xpeer(d)).wait_recv()
        ar_copy(ar_b, yfrom(d), 4 + d, ypeer(d)).wait_recv()
    ar_c[leaf] = (ar_a[0] + ar_a[1]) + (ar_a[2] + ar_a[3])
    ar_d[x] = (ar_b[0] + ar_b[1]) + (ar_b[2] + ar_b[3])
    for d in range(1, NX):
        ar_copy(ar_c, leaf, 8 + d, ypeer(d)).start()
        ar_copy(ar_d, x, 12 + d, xpeer(d)).start()

    swap_z.wait()
    mine, theirs = zback[...], zbuf[...]
    entry = jnp.concatenate([jnp.where(first, mine, theirs), jnp.where(first, theirs, mine)], axis=0)
    inner = ex_r[...] + nt(entry, a0[...])
    entry = jnp.where(first, entry, inner)
    chain_inverse = split(inverse[LOC])
    bt[...] = nn(nt(rt[...] - entry, chain_inverse), chain_inverse)
    m_s[...] = jnp.where(first, bt[...], nn(bt[...], a0[...]))
    swap_m = swap(m_s, m_r, 3)
    swap_m.start()
    swap_m.wait()
    bchip[...] = m_s[half] + m_r[half]

    def b_copy(d):
        to = lax.rem(z + d, NZ)
        return copy(bchip.at[rows_of(to)], bbuf.at[z], b_s.at[d], b_r.at[d], zpeer(d))

    for d in order:
        b_copy(d).start()
    bbuf[z] = bchip[rows_of(z)]

    for d in range(1, NX):
        ar_copy(ar_c, yfrom(d), 8 + d, ypeer(d)).wait_recv()
        ar_copy(ar_d, xfrom(d), 12 + d, xpeer(d)).wait_recv()
    low = (ar_c[0] + ar_c[1]) + (ar_c[2] + ar_c[3])
    high = (ar_d[0] + ar_d[1]) + (ar_d[2] + ar_d[3])
    mine_rows = pl.ds(pl.multiple_of(q * H + z * Q, Q), Q)

    sums = [low[0], low[1], high[0], high[1]]
    forward = []
    for t in range(TOP):
        value = nt(trt[t, mine_rows] - sums[t], (tih[t], til[t]))
        if t > 0:
            value = value - nt(forward[-1], (kh[t - 1], kl[t - 1]))
        forward.append(value)
    above = None
    found = [None] * TOP
    for t in reversed(range(TOP)):
        value = nn(forward[t], (tih[t], til[t]))
        if t < TOP - 1:
            value = value - nn(above, (lh[t], ll[t]))
        above = value
        found[t] = value
        topx[t] = value

    def tp_copy(d):
        return copy(topx, topt.at[:, mine_rows], tp_s.at[d], tp_r.at[d], zpeer(d))

    for d in order:
        tp_copy(d).start()
    topt[:, mine_rows] = topx[...]

    found_h, found_l = split(jnp.concatenate(found, axis=1))
    picked = once(found_h, pall[...], ((1,), (0,))) + once(found_l, pall[...], ((1,), (0,)))
    for d in order:
        copy(bchip.at[pl.ds(0, Q)], bbuf.at[zfrom(d)], b_s.at[d], b_r.at[d], zpeer(d)).wait_recv()
    for c in range(NZ):
        reach = jnp.concatenate([vbuf[c, 0, pl.ds(0, 64)], vbuf[c, 1, pl.ds(0, 64)]], axis=0)
        z0[c] = bbuf[c] - nn(picked[:, c * H : (c + 1) * H], reach)

    def back(i, carry):
        c = NZ - 1 - i
        z0[c] = z0[c] + nt(z0[c + 1], (ach[c], acl[c]))
        return carry

    lax.fori_loop(1, NZ, back, 0)

    hop_b = copy(xout_b, xin_b, xb_s.at[0], xb_r.at[0], at(lax.rem(x + NX - 1, NX), z, q))

    @pl.when(x == NX - 1)
    def _():
        xin_b[...] = jnp.zeros((Q, W), F32)
        xout_b[...] = z0[0]

    @pl.when(x < NX - 1)
    def _():
        hop_b.wait_recv()
        xout_b[...] = z0[0] + nt(xin_b[...], (fh[NZ - 1], fl[NZ - 1]))

    @pl.when(x > 0)
    def _():
        hop_b.start()

    leaving = split(xin_b[...])
    xsend[NZ - 1] = xin_b[...]

    def unfix(c, carry):
        xsend[c] = z0[c + 1] + nt(leaving, (gh[c + 1], gl[c + 1]))
        return carry

    lax.fori_loop(0, NZ - 1, unfix, 0)

    def xa_copy(d):
        to = lax.rem(z + d, NZ)
        return copy(xsend.at[to], xback.at[rows_of(z)], xa_s.at[d], xa_r.at[d], zpeer(d))

    for d in order:
        xa_copy(d).start()
    xback[rows_of(z)] = xsend[z]

    for d in order:
        place = pl.ds(pl.multiple_of(q * H + zfrom(d) * Q, Q), Q)
        copy(topx, topt.at[:, place], tp_s.at[d], tp_r.at[d], zpeer(d)).wait_recv()
    swap_t = copy(topt.at[:, half], topt.at[:, half], up_s.at[1], up_r.at[1], sibling)
    swap_t.start()
    swap_t.wait_send()
    copy(topt.at[:, other], topt.at[:, other], up_s.at[1], up_r.at[1], sibling).wait_recv()
    bt[...] = bt[...] - nn(topt[target[0]], nfull[...])
    mb_s[...] = nn(bt[...], a0[...])
    swap_b = swap(mb_s, mb_r, 4)
    swap_b.start()
    for t in range(TOP):
        top_out[t] = topt[t].T

    def lower(k, carry):
        hval[k] = hval[k] - tn((ddh[k], ddl[k]), top_out[links[k, 1]])
        return carry

    lax.fori_loop(0, LOC, lower, 0)
    swap_b.wait()
    base = bt[...] + jnp.where(first, mb_r[...], 0.0)

    for d in order:
        copy(xsend.at[0], xback.at[rows_of(zfrom(d))], xa_s.at[d], xa_r.at[d], zpeer(d)).wait_recv()
    swap_x = swap(xback, zbuf, 5)
    swap_x.start()
    swap_x.wait()
    mine, theirs = xback[...], zbuf[...]
    exits = jnp.concatenate([jnp.where(first, mine, theirs), jnp.where(first, theirs, mine)], axis=0)
    out[LOC] = (base + nn(exits, msel[...])).T

    def local_back(i, carry):
        k = LOC - 1 - i
        out[k] = hval[k] - tn((dh[k], dl[k]), out[links[k, 0]])
        return carry

    lax.fori_loop(0, LOC, local_back, 0)

    for d in order:
        ac_copy(d).wait_send()
        v_copy(d).wait_send()
        ac_pass(d).wait_send()
        v_pass(d).wait_send()
        s_copy(d).wait_send()
        zr_copy(d).wait_send()
        zb_copy(d).wait_send()
        b_copy(d).wait_send()
        tp_copy(d).wait_send()
        xa_copy(d).wait_send()
    v_own.wait_send()
    for d in range(1, NX):
        y_copy(d).wait_send()
        ar_copy(ar_a, x, d, xpeer(d)).wait_send()
        ar_copy(ar_b, leaf, 4 + d, ypeer(d)).wait_send()
        ar_copy(ar_c, leaf, 8 + d, ypeer(d)).wait_send()
        ar_copy(ar_d, x, 12 + d, xpeer(d)).wait_send()

    @pl.when(x < NX - 1)
    def _():
        hop_f.wait_send()

    @pl.when(x > 0)
    def _():
        hop_b.wait_send()


def shards(
    node_rhs, node_inverse, local_blocks, chain_next, chain_top, top_rhs, top_inverse, top_next,
    ancestors, block_rows, chain_target, chain_rows,
):
    vmem = pl.BlockSpec(memory_space=pltpu.VMEM)
    smem = pl.BlockSpec(memory_space=pltpu.SMEM)

    def f32(*shape):
        return pltpu.VMEM(shape, F32)

    def b16(*shape):
        return pltpu.VMEM(shape, BF16)

    def sem(count):
        return pltpu.SemaphoreType.DMA((count,))

    scratch = [
        f32(LOC + 1, W, W), b16(LOC, W, W), b16(LOC, W, W), b16(LOC, W, W), b16(LOC, W, W), f32(LOC, W, W),
        f32(TOP, W, W), f32(TOP, W, W), f32(TOP, H, W), f32(TOP, H, W), f32(NY, H, W), f32(H, W), f32(NZ, Q, W),
        f32(W, W), f32(W, W), f32(W, W), f32(W, W), f32(W, W), f32(W, W),
        f32(NZ, W, W), b16(NZ, W, W), b16(NZ, W, W), b16(NZ, W, W), b16(NZ, W, W), b16(NZ, W, W), b16(NZ, W, W),
        f32(NZ, 2, 72, W), b16(TOP * W, NZ * H),
        f32(W, W), f32(W, W), f32(W, W), f32(H, W), f32(NZ, Q, W), f32(NZ, Q, W), f32(NZ, Q, W), f32(H, W),
        f32(H, W), f32(Q, W), f32(Q, W),
        f32(NX, 2, Q, W), f32(NY, 2, Q, W), f32(NY, 2, Q, W), f32(NX, 2, Q, W),
        f32(TOP, Q, W), f32(TOP, W, W), f32(TOP, W, W), b16(TOP, W, W), b16(TOP, W, W),
        b16(TOP - 1, W, W), b16(TOP - 1, W, W), b16(TOP - 1, W, W), b16(TOP - 1, W, W),
        f32(W, W), f32(W, W), f32(W, W), f32(H, W), f32(NZ, Q, W), f32(NZ, Q, W), f32(H, W),
        f32(Q, W), f32(Q, W), f32(W, W), f32(W, W),
        sem(6), sem(6), sem(8), sem(8), sem(8), sem(8), sem(8), sem(8), sem(8), sem(8), sem(1), sem(1),
        sem(8), sem(8), sem(2), sem(2), sem(4), sem(4), sem(8), sem(8), sem(1), sem(1), sem(8), sem(8),
        sem(16), sem(16), sem(8), sem(8), sem(1), sem(1), sem(8), sem(8), sem(8), sem(8),
    ]
    solved, top = pl.pallas_call(
        kernel,
        out_shape=(
            jax.ShapeDtypeStruct((LOC + 1, W, W), F32),
            jax.ShapeDtypeStruct((TOP, W, W), F32),
        ),
        in_specs=[smem, smem] + [vmem] * 10,
        out_specs=(vmem, vmem),
        scratch_shapes=scratch,
        compiler_params=pltpu.CompilerParams(
            collective_id=0, has_side_effects=True, vmem_limit_bytes=56 * 1024 * 1024
        ),
    )(
        ancestors[0, 0],
        chain_target[0],
        node_rhs[0, 0],
        node_inverse[0, 0],
        local_blocks[0, 0].reshape(LOC, 128, W),
        chain_next[0, 0],
        chain_top[0, 0],
        top_rhs,
        top_inverse,
        top_next,
        block_rows[0, 0].reshape(2 * LOC, 64),
        chain_rows[0],
    )
    return solved[None, None], top


def solution(mesh):
    placed = (
        P("leaf", "col", None, None, None),
        P("leaf", "col", None, None, None),
        P("leaf", "col", None, None, None, None),
        P("leaf", "col", None, None),
        P("leaf", "col", None, None),
        P(),
        P(),
        P(),
        P("leaf", "col", None, None),
        P("leaf", "col", None, None, None),
        P("leaf", "col"),
        P("leaf", "col", None),
    )
    return jax.shard_map(
        shards,
        mesh=mesh,
        in_specs=placed,
        out_specs=(P("leaf", "col", None, None, None), P()),
        check_vma=False,
    )
```

time: 1180 us -> 123 us (0.10); the launches traced: 1160 us -> 123 us
  waiting for transfers between devices: 548 us -> 0 us
  matrix products: 305 us -> 0 us
  local copies, waits for them, and re-layouts: 171 us -> 5.63 us
  Pallas kernels: 0 us -> 116 us
  other arithmetic: 88.5 us -> 0 us
  between operations: 45.8 us -> 1.29 us
    dot_general x196 -> x0, matrix products: 305 us -> none  [the longest x162 273 us: product(): jnp.dot(left, right, precision=precise, preferred_element_type=jnp.float32)]
    all_gather x4 -> x0, waiting for transfers between devices: 296 us -> none  [prefix(): pieces = jax.tree.map(lambda part: lax.all_gather(part, axis), value)]
    psum x1 -> x0, waiting for transfers between devices: 251 us -> none  [shards(): summed = lax.psum(upward, ('leaf', 'col'))]
    pallas_call x0 -> x1, Pallas kernels: none -> 116 us  [shards(): pl.pallas_call(kernel, out_shape=(jax.ShapeDtypeStruct((LOC + 1, W, W), F...]
    scatter-add x17 -> x0, other arithmetic: 85.9 us -> none  [the longest x8 41.1 us: local_forward(): pending.at[links[member, 0], row_index[member, 0]]]
    while x126 -> x0, local copies, waits for them, and re-layouts: 61 us -> none
    all_gather x2 -> x0, local copies, waits for them, and re-layouts: 35.3 us -> none  [prefix(): pieces = jax.tree.map(lambda part: lax.all_gather(part, axis), value)]
    gather x17 -> x0, local copies, waits for them, and re-layouts: 29.9 us -> none  [the longest x8 16.8 us: local_backward(): above_rows = known_values[links[member, 0], row_index[member, 0]]]
  transfers between devices with their start and end apart: 5 -> 0, of which waited for: 5 -> 0; matrix products, arithmetic and copies ran while one was open for 10% -> 0% of each run, Pallas kernels for 0% -> 0%
where the time goes in v1:
time: 123 us
  Pallas kernels  116 us (94%)
  local copies, waits for them, and re-layouts  5.63 us (5%)
  between operations  1.29 us (1%)
    pallas_call x1, Pallas kernels, shards(): pl.pallas_call(kernel, out_shape=(jax.ShapeDtypeStruct((LOC + 1, W, W), F...  116 us
    unnamed x4, local copies, waits for them, and re-layouts  4.28 us

profile of v1, /device:TPU:1, one launch (start us, length us, event | category | flops | bytes accessed | tf_op | source)
XLA Modules:
  0.0 123.1 jit_solution(13920970051975712406)
XLA Ops:
  1.3 1.3 %copy.14.links = s32[8,2]{1,0:T(8,128)} copy(s32[8,2]{0,1:T(2,128)} %bitcast.18) | data formatting | bytes 128 | tf_op jit(solution)/shard_map/squeeze | solution.py:600
  2.6 116.2 %shard_map.131 = (f32[9,256,256]{2,1,0:T(8,128)}, f32[4,256,256]{2,1,0:T(8,128)}) custom-call(s32[8,2]{1,0:T(8,128)} %copy.14.links, s32[1]{0:T(128)} %bitcast.10.target, f32[9,256,256]{2,1,0:T(8,128)} %bitcast.11, f32[9,256,256]{2,1,0:T(8,128)} %bitcast.12, f32[8,128,256]{2,1,0:T(8,128)} %bitcast.14, f32[256,256]{1,0:T(8,128)} %bitcast.15, ...), custom_call_target="tpu_custom_call" | custom-call | tf_op jit(solution)/shard_map/pallas_call | solution.py:587
  118.8 0.0 copy-start
  118.8 3.3 %copy.18 = f32[1,1,9,256,256]{4,3,2,1,0:T(8,128)} copy(f32[1,1,9,256,256]{4,3,2,1,0:T(8,128)} %bitcast.13) | data formatting | bytes 4718592
  122.1 0.0 copy-done
  122.1 1.0 copy.19
Async XLA Ops:
  118.8 3.3 %copy-start = (f32[4,256,256]{2,1,0:T(8,128)S(1)}, f32[4,256,256]{2,1,0:T(8,128)}, u32[]{:S(2)}) copy-start(f32[4,256,256]{2,1,0:T(8,128)} %get-tuple-element.9) | copy-start | bytes 3145732

commit v2 on v1

--- a/solution.py
+++ b/solution.py
@@ -51,14 +51,15 @@
 
 
 def kernel(
-    links, target, rhs, inverse, blocks, onward, sideways, top_rhs, top_inverse, top_next, rows, chain_rows,
-    out, top_out,
-    src, dh, dl, ddh, ddl, hval, upn, upt, uprecv, uph, ybuf, uy, zred,
-    a_own, a_sib, a0, a1, msel, nfull, acf, ach, acl, fh, fl, gh, gl, vbuf, pall,
+    links, target, rhs_in, inverse_in, blocks_in, onward, sideways, top_rhs_in, top_inverse_in, top_next_in, rows, chain_rows,
+    out_to, top_to,
+    src, inverse, blocks, top_rhs, top_inverse, top_next, out, top_out,
+    dh, dl, n1h, n1l, ycat, pt, hval, upt, uprecv, uph, ybuf, uy, zred,
+    a_own, a_sib, a0, a1, msel, side_v, acf, ach, acl, fh, fl, gh, gl, vbuf, pall,
     rt, ex_s, ex_r, schip, sbuf, z0, zsend, zbuf, zback, xin_f, xout_f,
     ar_a, ar_b, ar_c, ar_d, topx, topt, trt, tih, til, kh, kl, lh, ll,
     bt, m_s, m_r, bchip, bbuf, xsend, xback, xin_b, xout_b, mb_s, mb_r,
-    core_s, core_r, ac_s, ac_r, acx_s, acx_r, v_s, v_r, vx_s, vx_r, vo_s, vo_r,
+    load, store, core_s, core_r, ac_s, ac_r, acx_s, acx_r, v_s, v_r, vx_s, vx_r, vo_s, vo_r,
     s_s, s_r, up_s, up_r, y_s, y_r, zr_s, zr_r, xf_s, xf_r, zb_s, zb_r, ar_s, ar_r,
     b_s, b_r, xb_s, xb_r, xa_s, xa_r, tp_s, tp_r,
 ):
@@ -103,6 +104,18 @@
     for peer in peers:
         pl.semaphore_signal(barrier, inc=1, device_id=peer, device_id_type=MESH)
 
+    loads = [
+        pltpu.make_async_copy(inverse_in.at[LOC], inverse.at[LOC], load.at[0]),
+        pltpu.make_async_copy(inverse_in.at[pl.ds(0, LOC)], inverse.at[pl.ds(0, LOC)], load.at[1]),
+        pltpu.make_async_copy(blocks_in, blocks, load.at[2]),
+        pltpu.make_async_copy(rhs_in, src, load.at[3]),
+        pltpu.make_async_copy(top_inverse_in, top_inverse, load.at[4]),
+        pltpu.make_async_copy(top_next_in, top_next, load.at[5]),
+        pltpu.make_async_copy(top_rhs_in, top_rhs, load.at[6]),
+    ]
+    for item in loads:
+        item.start()
+
     first = q == 0
     half = pl.ds(pl.multiple_of(q * H, H), H)
     other = pl.ds(pl.multiple_of((1 - q) * H, H), H)
@@ -110,37 +123,88 @@
     def rows_of(zz):
         return pl.ds(pl.multiple_of(zz * Q, Q), Q)
 
+    def by_four(body):
+        def four(i, carry):
+            for j in range(4):
+                body(4 * i + j)
+            return carry
+
+        lax.fori_loop(0, 2, four, 0)
+
+    loads[0].wait()
     chain_inverse = split(inverse[LOC])
     coupling = jnp.where(col == NCOL - 1, jnp.zeros((W, W), F32), onward[...])
     a_own[...] = -nn(coupling, chain_inverse)
-    side = nn(sideways[...], chain_inverse)
-    side_h, side_l = split(side)
-    spread = one_hot(chain_rows[...], W)
-    nfull[...] = once(spread, side_h, ((1,), (0,))) + once(spread, side_l, ((1,), (0,)))
-
     pl.semaphore_wait(barrier, len(peers))
     swap_a = swap(a_own, a_sib, 0)
     swap_a.start()
-
-    def local_map(k, carry):
+    side = nn(sideways[...], chain_inverse)
+    side_v[...] = side
+    loads[1].wait()
+    loads[2].wait()
+
+    def local_map(k):
         near = nn(blocks[k], inverse[k])
         near_h, near_l = split(near)
         to_parent = one_hot(rows[pl.ds(2 * k, 1), :], W)
-        to_top = one_hot(rows[pl.ds(2 * k + 1, 1), :], W)
         dh[k] = once(to_parent, near_h[:64], ((1,), (0,))).astype(BF16)
         dl[k] = once(to_parent, near_l[:64], ((1,), (0,))).astype(BF16)
-        ddh[k] = once(to_top, near_h[64:], ((1,), (0,))).astype(BF16)
-        ddl[k] = once(to_top, near_l[64:], ((1,), (0,))).astype(BF16)
-        return carry
-
-    lax.fori_loop(0, LOC, local_map, 0)
-
-    swap_a.wait()
+        n1h[k] = near_h[64:]
+        n1l[k] = near_l[64:]
+
+    def some_maps(start):
+        def two(i, carry):
+            local_map(start + 2 * i)
+            local_map(start + 2 * i + 1)
+            return carry
+
+        lax.fori_loop(0, 2, two, 0)
+
+    swap_a.wait_recv()
     a0[...] = jnp.where(first, a_own[...], a_sib[...])
     a1[...] = jnp.where(first, a_sib[...], a_own[...])
     pair = nn(a1[...], a0[...])
+    acf[z] = pair.T
+
+    def ring_part(core, way, s, h):
+        slot = lax.rem(z + NZ - s * way, NZ)
+        return acf.at[slot, pl.ds(pl.multiple_of(core * H + h * 64, 64), 64)]
+
+    def ring_number(way, s, h):
+        return ((way + 1) // 2 * 4 + s) * 2 + h
+
+    def ring(way, s, h):
+        part, i = ring_part(q, way, s, h), ring_number(way, s, h)
+        return copy(part, part, ac_s.at[i], ac_r.at[i], zpeer(way % NZ))
+
+    def ring_in(way, s, h):
+        part, i = ring_part(q, way, s + 1, h), ring_number(way, s, h)
+        return copy(part, part, ac_s.at[i], ac_r.at[i], zpeer(way % NZ))
+
+    def ring_pass(way, s, h):
+        part, i = ring_part(q, way, s + 1, h), ring_number(way, s, h)
+        return copy(part, part, acx_s.at[i], acx_r.at[i], sibling)
+
+    def ring_passed(way, s, h):
+        part, i = ring_part(1 - q, way, s + 1, h), ring_number(way, s, h)
+        return copy(part, part, acx_s.at[i], acx_r.at[i], sibling)
+
+    moves = [[(way, s, h) for h in range(2) for way in (1, -1)] for s in range(3)]
+    moves.append([(1, 3, 0), (-1, 3, 1)])
+
+    def ring_step(s):
+        if s > 0:
+            for way, _, h in moves[s - 1]:
+                ring_in(way, s - 1, h).wait_recv()
+                if s < 4 and (way, s, h) in moves[s]:
+                    ring(way, s, h).start()
+                ring_pass(way, s - 1, h).start()
+        else:
+            for way, _, h in moves[0]:
+                ring(way, 0, h).start()
+
+    ring_step(0)
     msel[...] = jnp.where(first, pair, a_own[...])
-    acf[z] = pair.T
     vbuf[z, q, pl.ds(0, 64)] = jnp.where(first, side, nn(side, a0[...]))
     index = (chain_rows[...] + target[0] * W).astype(F32)
     empty = jnp.zeros((1, 64), F32)
@@ -149,32 +213,32 @@
     )
     vbuf[z, q, pl.ds(64, 8)] = jnp.broadcast_to(index, (8, W))
 
-    def ac_copy(d):
-        return copy(acf.at[z, half], acf.at[z, half], ac_s.at[d], ac_r.at[d], zpeer(d))
-
     def v_copy(d):
         return copy(vbuf.at[z, q], vbuf.at[z, q], v_s.at[d], v_r.at[d], zpeer(d))
 
     order = (1, 7, 2, 6, 3, 5, 4)
-    for d in order:
-        ac_copy(d).start()
     v_own = copy(vbuf.at[z, q], vbuf.at[z, q], vo_s.at[0], vo_r.at[0], sibling)
     v_own.start()
-    for d in order:
-        v_copy(d).start()
-
-    for k in range(LOC + 1):
-        src[k] = rhs[k]
+    some_maps(0)
+    ring_step(1)
+    some_maps(4)
+    ring_step(2)
+    loads[3].wait()
+
     for k in range(LOC):
         update = nn((dh[k], dl[k]), src[k])
         for j in range(k + 1, LOC + 1):
-            src[j] = src[j] - jnp.where(links[k, 0] == j, update, 0.0)
+            src[j] = src[j] - jnp.where(links[0, k] == j, update, 0.0)
+        if k == 2:
+            ring_step(3)
+        if k == 6:
+            ring_step(4)
 
     rt[...] = src[LOC].T
     ex_s[...] = jnp.where(first, -nt(rt[...], a_own[...]), rt[...])
     swap_s = swap(ex_s, ex_r, 1)
     swap_s.start()
-    swap_s.wait()
+    swap_s.wait_recv()
     shift_half = jnp.where(first, ex_s[half], ex_r[half])
     rest_half = jnp.where(first, ex_r[half], ex_s[half])
     schip[...] = -nt(rest_half - shift_half, a1[...])
@@ -187,40 +251,39 @@
         s_copy(d).start()
     sbuf[z] = schip[rows_of(z)]
 
+    for d in order:
+        v_copy(d).start()
+
+    def up_part(k):
+        ycat[pl.ds(pl.multiple_of(k * 64, 64), 64)] = nn((n1h[k], n1l[k]), src[k])
+
+    by_four(up_part)
+    diagonal = lax.broadcasted_iota(jnp.int32, (64, 64), 0) == lax.broadcasted_iota(jnp.int32, (64, 64), 1)
+
+    def places_of(index_row):
+        column = jnp.sum(jnp.where(diagonal, index_row, 0.0), axis=1, keepdims=True).astype(jnp.int32)
+        place = lax.broadcasted_iota(jnp.int32, (64, TOP * W), 1)
+        return jnp.where(place == column, 1.0, 0.0).astype(BF16)
+
+    def places_body(k):
+        index_row = (rows[pl.ds(2 * k + 1, 1), :] + links[1, k] * W).astype(F32)
+        pt[pl.ds(pl.multiple_of(k * 64, 64), 64)] = places_of(index_row)
+
+    by_four(places_body)
+    pt[pl.ds(512, 64)] = places_of((chain_rows[...] + target[0] * W).astype(F32))
+    up_h, up_l = split(ycat[...].T)
+    chain_h, chain_l = split(nt(jnp.where(first, rt[...], rt[...] - ex_r[...]), side_v[...]))
     for t in range(TOP):
-        upn[t] = jnp.zeros((W, W), F32)
-
-    def local_up(k, carry):
-        part = nn((ddh[k], ddl[k]), src[k])
-        for t in range(TOP):
-            upn[t] = upn[t] + jnp.where(links[k, 1] == t, part, 0.0)
-        return carry
-
-    lax.fori_loop(0, LOC, local_up, 0)
-    chain_part = nt(jnp.where(first, rt[...], rt[...] - ex_r[...]), nfull[...])
-    for t in range(TOP):
-        upt[t] = upn[t].T + jnp.where(target[0] == t, chain_part, 0.0)
+        here = pl.ds(t * W, W)
+        near, far = pt[pl.ds(0, 512), here], pt[pl.ds(512, 64), here]
+        near = once(up_h, near, ((1,), (0,))) + once(up_l, near, ((1,), (0,)))
+        far = once(chain_h, far, ((1,), (0,))) + once(chain_l, far, ((1,), (0,)))
+        upt[t] = near + far
     swap_u = copy(upt.at[:, other], uprecv, up_s.at[0], up_r.at[0], sibling)
     swap_u.start()
 
-    def square(k, carry):
-        here = split(inverse[k])
-        hval[k] = tn(here, nn(here, src[k]))
-        return carry
-
-    lax.fori_loop(0, LOC // 2, square, 0)
-    swap_u.wait()
-    for t in range(TOP):
-        uph[t] = upt[t, half] + uprecv[t]
-
-    def y_copy(d):
-        return copy(uph.at[lax.rem(leaf + d, NY)], ybuf.at[leaf], y_s.at[d], y_r.at[d], ypeer(d))
-
-    for d in range(1, NY):
-        y_copy(d).start()
-    ybuf[leaf] = uph[leaf]
-    lax.fori_loop(LOC // 2, LOC, square, 0)
-
+    for item in loads[4:]:
+        item.wait()
     for t in range(TOP):
         th, tl = split(top_inverse[t])
         tih[t] = th
@@ -229,18 +292,20 @@
     for t in range(TOP - 1):
         kh[t], kl[t] = split(nn((tih[t + 1], til[t + 1]), top_next[t]))
         lh[t], ll[t] = split(nn(top_next[t], (tih[t], til[t])))
-
-    def ac_pass(d):
-        part = acf.at[zfrom(d), half]
-        return copy(part, part, acx_s.at[d], acx_r.at[d], sibling)
-
-    def ac_come(d):
-        part = acf.at[zfrom(d), half]
-        return copy(part, part, ac_s.at[d], ac_r.at[d], zpeer(d))
-
-    def ac_passed(d):
-        part = acf.at[zfrom(d), other]
-        return copy(part, part, acx_s.at[d], acx_r.at[d], sibling)
+    swap_u.wait_recv()
+    for t in range(TOP):
+        uph[t] = upt[t, half] + uprecv[t]
+
+    def y_copy(d):
+        return copy(uph.at[lax.rem(leaf + d, NY)], ybuf.at[leaf], y_s.at[d], y_r.at[d], ypeer(d))
+
+    for d in range(1, NY):
+        y_copy(d).start()
+    ybuf[leaf] = uph[leaf]
+
+    def square(k):
+        here = split(inverse[k])
+        hval[k] = tn(here, nn(here, src[k]))
 
     def v_come(d):
         part = vbuf.at[zfrom(d), q]
@@ -254,22 +319,9 @@
         part = vbuf.at[zfrom(d), 1 - q]
         return copy(part, part, vx_s.at[d], vx_r.at[d], sibling)
 
-    for d in order:
-        ac_come(d).wait_recv()
-        ac_pass(d).start()
-    for d in range(1, NY):
-        copy(uph.at[0], ybuf.at[yfrom(d)], y_s.at[d], y_r.at[d], ypeer(d)).wait_recv()
-    uy[...] = (ybuf[0] + ybuf[1]) + (ybuf[2] + ybuf[3])
-
-    def zr_copy(d):
-        to = lax.rem(z + d, NZ)
-        return copy(uy.at[rows_of(to)], zred.at[z], zr_s.at[d], zr_r.at[d], zpeer(d))
-
-    for d in order:
-        zr_copy(d).start()
-    zred[z] = uy[rows_of(z)]
-    for d in order:
-        ac_passed(d).wait_recv()
+    for step in moves:
+        for move in step:
+            ring_passed(*move).wait_recv()
 
     def halves(c, carry):
         ach[c], acl[c] = split(acf[c])
@@ -291,6 +343,10 @@
 
     lax.fori_loop(1, NZ, prefix, 0)
 
+    @pl.when(x >= 2)
+    def _():
+        by_four(square)
+
     whole = (fh[NZ - 1], fl[NZ - 1])
     hop_f = copy(xout_f, xin_f, xf_s.at[0], xf_r.at[0], at(lax.rem(x + 1, NX), z, q))
 
@@ -307,6 +363,22 @@
     @pl.when(x < NX - 1)
     def _():
         hop_f.start()
+
+    for d in range(1, NY):
+        copy(uph.at[0], ybuf.at[yfrom(d)], y_s.at[d], y_r.at[d], ypeer(d)).wait_recv()
+    uy[...] = (ybuf[0] + ybuf[1]) + (ybuf[2] + ybuf[3])
+
+    def zr_copy(d):
+        to = lax.rem(z + d, NZ)
+        return copy(uy.at[rows_of(to)], zred.at[z], zr_s.at[d], zr_r.at[d], zpeer(d))
+
+    for d in order:
+        zr_copy(d).start()
+    zred[z] = uy[rows_of(z)]
+
+    @pl.when(x < 2)
+    def _():
+        by_four(square)
 
     entering = split(xin_f[...])
     zsend[0] = xin_f[...]
@@ -385,7 +457,7 @@
         ar_copy(ar_c, leaf, 8 + d, ypeer(d)).start()
         ar_copy(ar_d, x, 12 + d, xpeer(d)).start()
 
-    swap_z.wait()
+    swap_z.wait_recv()
     mine, theirs = zback[...], zbuf[...]
     entry = jnp.concatenate([jnp.where(first, mine, theirs), jnp.where(first, theirs, mine)], axis=0)
     inner = ex_r[...] + nt(entry, a0[...])
@@ -395,7 +467,7 @@
     m_s[...] = jnp.where(first, bt[...], nn(bt[...], a0[...]))
     swap_m = swap(m_s, m_r, 3)
     swap_m.start()
-    swap_m.wait()
+    swap_m.wait_recv()
     bchip[...] = m_s[half] + m_r[half]
 
     def b_copy(d):
@@ -452,6 +524,38 @@
 
     lax.fori_loop(1, NZ, back, 0)
 
+    swap_t = copy(topt.at[:, half], topt.at[:, half], up_s.at[1], up_r.at[1], sibling)
+    swap_b = swap(mb_s, mb_r, 4)
+
+    def with_top():
+        for d in order:
+            place = pl.ds(pl.multiple_of(q * H + zfrom(d) * Q, Q), Q)
+            copy(topx, topt.at[:, place], tp_s.at[d], tp_r.at[d], zpeer(d)).wait_recv()
+        swap_t.start()
+        copy(topt.at[:, other], topt.at[:, other], up_s.at[1], up_r.at[1], sibling).wait_recv()
+        pick, pick_chain = 0.0, 0.0
+        for t in range(TOP):
+            here = pl.ds(t * W, W)
+            value = topt[t].T
+            top_out[t] = value
+            vh, vl = split(value)
+            near, far = pt[pl.ds(0, 512), here], pt[pl.ds(512, 64), here]
+            pick = pick + (once(near, vh, ((1,), (0,))) + once(near, vl, ((1,), (0,))))
+            pick_chain = pick_chain + (once(far, vh, ((1,), (0,))) + once(far, vl, ((1,), (0,))))
+        ycat[...] = pick
+        bt[...] = bt[...] - tn(pick_chain, side_v[...])
+        mb_s[...] = nn(bt[...], a0[...])
+        swap_b.start()
+
+        def lower(k):
+            hval[k] = hval[k] - tn((n1h[k], n1l[k]), ycat[pl.ds(pl.multiple_of(k * 64, 64), 64)])
+
+        by_four(lower)
+
+    @pl.when(x == 0)
+    def _():
+        with_top()
+
     hop_b = copy(xout_b, xin_b, xb_s.at[0], xb_r.at[0], at(lax.rem(x + NX - 1, NX), z, q))
 
     @pl.when(x == NX - 1)
@@ -485,48 +589,36 @@
         xa_copy(d).start()
     xback[rows_of(z)] = xsend[z]
 
-    for d in order:
-        place = pl.ds(pl.multiple_of(q * H + zfrom(d) * Q, Q), Q)
-        copy(topx, topt.at[:, place], tp_s.at[d], tp_r.at[d], zpeer(d)).wait_recv()
-    swap_t = copy(topt.at[:, half], topt.at[:, half], up_s.at[1], up_r.at[1], sibling)
-    swap_t.start()
-    swap_t.wait_send()
-    copy(topt.at[:, other], topt.at[:, other], up_s.at[1], up_r.at[1], sibling).wait_recv()
-    bt[...] = bt[...] - nn(topt[target[0]], nfull[...])
-    mb_s[...] = nn(bt[...], a0[...])
-    swap_b = swap(mb_s, mb_r, 4)
-    swap_b.start()
-    for t in range(TOP):
-        top_out[t] = topt[t].T
-
-    def lower(k, carry):
-        hval[k] = hval[k] - tn((ddh[k], ddl[k]), top_out[links[k, 1]])
-        return carry
-
-    lax.fori_loop(0, LOC, lower, 0)
-    swap_b.wait()
+    @pl.when(x > 0)
+    def _():
+        with_top()
+
+    top_store = pltpu.make_async_copy(top_out, top_to, store.at[LOC + 1])
+    top_store.start()
+    swap_b.wait_recv()
     base = bt[...] + jnp.where(first, mb_r[...], 0.0)
-
     for d in order:
         copy(xsend.at[0], xback.at[rows_of(zfrom(d))], xa_s.at[d], xa_r.at[d], zpeer(d)).wait_recv()
     swap_x = swap(xback, zbuf, 5)
     swap_x.start()
-    swap_x.wait()
+    swap_x.wait_recv()
     mine, theirs = xback[...], zbuf[...]
     exits = jnp.concatenate([jnp.where(first, mine, theirs), jnp.where(first, theirs, mine)], axis=0)
     out[LOC] = (base + nn(exits, msel[...])).T
 
-    def local_back(i, carry):
-        k = LOC - 1 - i
-        out[k] = hval[k] - tn((dh[k], dl[k]), out[links[k, 0]])
-        return carry
-
-    lax.fori_loop(0, LOC, local_back, 0)
-
-    for d in order:
-        ac_copy(d).wait_send()
+    def keep(k):
+        return pltpu.make_async_copy(out.at[k], out_to.at[k], store.at[k])
+
+    keep(LOC).start()
+    for k in reversed(range(LOC)):
+        out[k] = hval[k] - tn((dh[k], dl[k]), out[links[0, k]])
+        keep(k).start()
+    for k in range(LOC + 1):
+        keep(k).wait()
+    top_store.wait()
+
+    for d in order:
         v_copy(d).wait_send()
-        ac_pass(d).wait_send()
         v_pass(d).wait_send()
         s_copy(d).wait_send()
         zr_copy(d).wait_send()
@@ -535,6 +627,12 @@
         tp_copy(d).wait_send()
         xa_copy(d).wait_send()
     v_own.wait_send()
+    for step in moves:
+        for move in step:
+            ring(*move).wait_send()
+            ring_pass(*move).wait_send()
+    for item in (swap_a, swap_s, swap_u, swap_z, swap_m, swap_t, swap_b, swap_x):
+        item.wait_send()
     for d in range(1, NX):
         y_copy(d).wait_send()
         ar_copy(ar_a, x, d, xpeer(d)).wait_send()
@@ -557,6 +655,7 @@
 ):
     vmem = pl.BlockSpec(memory_space=pltpu.VMEM)
     smem = pl.BlockSpec(memory_space=pltpu.SMEM)
+    hbm = pl.BlockSpec(memory_space=pl.ANY)
 
     def f32(*shape):
         return pltpu.VMEM(shape, F32)
@@ -568,9 +667,11 @@
         return pltpu.SemaphoreType.DMA((count,))
 
     scratch = [
-        f32(LOC + 1, W, W), b16(LOC, W, W), b16(LOC, W, W), b16(LOC, W, W), b16(LOC, W, W), f32(LOC, W, W),
-        f32(TOP, W, W), f32(TOP, W, W), f32(TOP, H, W), f32(TOP, H, W), f32(NY, H, W), f32(H, W), f32(NZ, Q, W),
-        f32(W, W), f32(W, W), f32(W, W), f32(W, W), f32(W, W), f32(W, W),
+        f32(LOC + 1, W, W), f32(LOC + 1, W, W), f32(LOC, 128, W), f32(TOP, W, W), f32(TOP, W, W),
+        f32(TOP - 1, W, W), f32(LOC + 1, W, W), f32(TOP, W, W),
+        b16(LOC, W, W), b16(LOC, W, W), b16(LOC, 64, W), b16(LOC, 64, W), f32(512, W), b16(576, TOP * W),
+        f32(LOC, W, W), f32(TOP, W, W), f32(TOP, H, W), f32(TOP, H, W), f32(NY, H, W), f32(H, W), f32(NZ, Q, W),
+        f32(W, W), f32(W, W), f32(W, W), f32(W, W), f32(W, W), f32(64, W),
         f32(NZ, W, W), b16(NZ, W, W), b16(NZ, W, W), b16(NZ, W, W), b16(NZ, W, W), b16(NZ, W, W), b16(NZ, W, W),
         f32(NZ, 2, 72, W), b16(TOP * W, NZ * H),
         f32(W, W), f32(W, W), f32(W, W), f32(H, W), f32(NZ, Q, W), f32(NZ, Q, W), f32(NZ, Q, W), f32(H, W),
@@ -580,7 +681,8 @@
         b16(TOP - 1, W, W), b16(TOP - 1, W, W), b16(TOP - 1, W, W), b16(TOP - 1, W, W),
         f32(W, W), f32(W, W), f32(W, W), f32(H, W), f32(NZ, Q, W), f32(NZ, Q, W), f32(H, W),
         f32(Q, W), f32(Q, W), f32(W, W), f32(W, W),
-        sem(6), sem(6), sem(8), sem(8), sem(8), sem(8), sem(8), sem(8), sem(8), sem(8), sem(1), sem(1),
+        sem(7), sem(LOC + 2), sem(6), sem(6), sem(16), sem(16), sem(16), sem(16), sem(8), sem(8), sem(8), sem(8),
+        sem(1), sem(1),
         sem(8), sem(8), sem(2), sem(2), sem(4), sem(4), sem(8), sem(8), sem(1), sem(1), sem(8), sem(8),
         sem(16), sem(16), sem(8), sem(8), sem(1), sem(1), sem(8), sem(8), sem(8), sem(8),
     ]
@@ -590,14 +692,14 @@
             jax.ShapeDtypeStruct((LOC + 1, W, W), F32),
             jax.ShapeDtypeStruct((TOP, W, W), F32),
         ),
-        in_specs=[smem, smem] + [vmem] * 10,
-        out_specs=(vmem, vmem),
+        in_specs=[smem, smem, hbm, hbm, hbm, vmem, vmem, hbm, hbm, hbm, vmem, vmem],
+        out_specs=(hbm, hbm),
         scratch_shapes=scratch,
         compiler_params=pltpu.CompilerParams(
             collective_id=0, has_side_effects=True, vmem_limit_bytes=56 * 1024 * 1024
         ),
     )(
-        ancestors[0, 0],
+        ancestors[0, 0].T,
         chain_target[0],
         node_rhs[0, 0],
         node_inverse[0, 0],

time: 123 us -> 102 us (0.83)
  Pallas kernels: 116 us -> 96.5 us
  local copies, waits for them, and re-layouts: 5.63 us -> 4.28 us
    pallas_call x1, Pallas kernels: 116 us -> 96.5 us  [shards(): pl.pallas_call(kernel, out_shape=(jax.ShapeDtypeStruct((LOC + 1, W, W), F...]
    squeeze x1 -> x0, local copies, waits for them, and re-layouts: 1.35 us -> none  [shards(): ancestors[0, 0]]
where the time goes in v2:
time: 102 us
  Pallas kernels  96.5 us (95%)
  local copies, waits for them, and re-layouts  4.28 us (4%)
  between operations  1.3 us (1%)
    pallas_call x1, Pallas kernels, shards(): pl.pallas_call(kernel, out_shape=(jax.ShapeDtypeStruct((LOC + 1, W, W), F...  96.5 us
    unnamed x4, local copies, waits for them, and re-layouts  4.28 us

profile of v2, /device:TPU:1, one launch (start us, length us, event | category | flops | bytes accessed | tf_op | source)
XLA Modules:
  0.0 102.1 jit_solution(8303111454988185318)
XLA Ops:
  1.3 96.5 %shard_map.131 = (f32[9,256,256]{2,1,0:T(8,128)}, f32[4,256,256]{2,1,0:T(8,128)}) custom-call(s32[2,8]{1,0:T(2,128)} %bitcast.20, s32[1]{0:T(128)} %bitcast.12.target, f32[9,256,256]{2,1,0:T(8,128)} %bitcast.14, f32[9,256,256]{2,1,0:T(8,128)} %bitcast.15, f32[8,128,256]{2,1,0:T(8,128)} %bitcast.16, f32[256,256]{1,0:T(8,128)} %bitcast.17, ...), custom_call_target="tpu_custom_call" | custom-call | tf_op jit(solution)/shard_map/pallas_call | solution.py:689
  97.8 0.0 copy-start
  97.8 3.3 %copy.17 = f32[1,1,9,256,256]{4,3,2,1,0:T(8,128)} copy(f32[1,1,9,256,256]{4,3,2,1,0:T(8,128)} %bitcast.13) | data formatting | bytes 4718592
  101.1 0.0 copy-done
  101.1 1.0 copy.18
Async XLA Ops:
  97.8 3.3 %copy-start = (f32[4,256,256]{2,1,0:T(8,128)S(1)}, f32[4,256,256]{2,1,0:T(8,128)}, u32[]{:S(2)}) copy-start(f32[4,256,256]{2,1,0:T(8,128)} %get-tuple-element.9) | copy-start | bytes 3145732

commit v3 on v2

--- a/solution.py
+++ b/solution.py
@@ -229,11 +229,8 @@
         update = nn((dh[k], dl[k]), src[k])
         for j in range(k + 1, LOC + 1):
             src[j] = src[j] - jnp.where(links[0, k] == j, update, 0.0)
-        if k == 2:
-            ring_step(3)
-        if k == 6:
-            ring_step(4)
-
+
+    ring_step(3)
     rt[...] = src[LOC].T
     ex_s[...] = jnp.where(first, -nt(rt[...], a_own[...]), rt[...])
     swap_s = swap(ex_s, ex_r, 1)
@@ -253,6 +250,8 @@
 
     for d in order:
         v_copy(d).start()
+
+    ring_step(4)
 
     def up_part(k):
         ycat[pl.ds(pl.multiple_of(k * 64, 64), 64)] = nn((n1h[k], n1l[k]), src[k])
@@ -343,42 +342,43 @@
 
     lax.fori_loop(1, NZ, prefix, 0)
 
-    @pl.when(x >= 2)
-    def _():
-        by_four(square)
-
-    whole = (fh[NZ - 1], fl[NZ - 1])
-    hop_f = copy(xout_f, xin_f, xf_s.at[0], xf_r.at[0], at(lax.rem(x + 1, NX), z, q))
-
-    @pl.when(x == 0)
-    def _():
-        xin_f[...] = jnp.zeros((Q, W), F32)
-        xout_f[...] = z0[NZ - 1]
-
-    @pl.when(x > 0)
-    def _():
-        hop_f.wait_recv()
-        xout_f[...] = z0[NZ - 1] + nn(xin_f[...], whole)
-
-    @pl.when(x < NX - 1)
-    def _():
-        hop_f.start()
-
-    for d in range(1, NY):
-        copy(uph.at[0], ybuf.at[yfrom(d)], y_s.at[d], y_r.at[d], ypeer(d)).wait_recv()
-    uy[...] = (ybuf[0] + ybuf[1]) + (ybuf[2] + ybuf[3])
-
     def zr_copy(d):
         to = lax.rem(z + d, NZ)
         return copy(uy.at[rows_of(to)], zred.at[z], zr_s.at[d], zr_r.at[d], zpeer(d))
 
-    for d in order:
-        zr_copy(d).start()
-    zred[z] = uy[rows_of(z)]
+    def aside():
+        for d in range(1, NY):
+            copy(uph.at[0], ybuf.at[yfrom(d)], y_s.at[d], y_r.at[d], ypeer(d)).wait_recv()
+        uy[...] = (ybuf[0] + ybuf[1]) + (ybuf[2] + ybuf[3])
+        for d in order:
+            zr_copy(d).start()
+        zred[z] = uy[rows_of(z)]
+        by_four(square)
+
+    @pl.when(x >= 2)
+    def _():
+        aside()
+
+    whole = (fh[NZ - 1], fl[NZ - 1])
+    hop_f = copy(xout_f, xin_f, xf_s.at[0], xf_r.at[0], at(lax.rem(x + 1, NX), z, q))
+
+    @pl.when(x == 0)
+    def _():
+        xin_f[...] = jnp.zeros((Q, W), F32)
+        xout_f[...] = z0[NZ - 1]
+
+    @pl.when(x > 0)
+    def _():
+        hop_f.wait_recv()
+        xout_f[...] = z0[NZ - 1] + nn(xin_f[...], whole)
+
+    @pl.when(x < NX - 1)
+    def _():
+        hop_f.start()
 
     @pl.when(x < 2)
     def _():
-        by_four(square)
+        aside()
 
     entering = split(xin_f[...])
     zsend[0] = xin_f[...]
@@ -528,6 +528,31 @@
     swap_b = swap(mb_s, mb_r, 4)
 
     def with_top():
+        for d in order:
+            v_copy(d).wait_send()
+            v_pass(d).wait_send()
+            s_copy(d).wait_send()
+            zr_copy(d).wait_send()
+            zb_copy(d).wait_send()
+            b_copy(d).wait_send()
+        v_own.wait_send()
+        for step in moves:
+            for move in step:
+                ring(*move).wait_send()
+                ring_pass(*move).wait_send()
+        for item in (swap_a, swap_s, swap_u, swap_z, swap_m):
+            item.wait_send()
+        for d in range(1, NX):
+            y_copy(d).wait_send()
+            ar_copy(ar_a, x, d, xpeer(d)).wait_send()
+            ar_copy(ar_b, leaf, 4 + d, ypeer(d)).wait_send()
+            ar_copy(ar_c, leaf, 8 + d, ypeer(d)).wait_send()
+            ar_copy(ar_d, x, 12 + d, xpeer(d)).wait_send()
+
+        @pl.when(x < NX - 1)
+        def _():
+            hop_f.wait_send()
+
         for d in order:
             place = pl.ds(pl.multiple_of(q * H + zfrom(d) * Q, Q), Q)
             copy(topx, topt.at[:, place], tp_s.at[d], tp_r.at[d], zpeer(d)).wait_recv()
@@ -618,31 +643,10 @@
     top_store.wait()
 
     for d in order:
-        v_copy(d).wait_send()
-        v_pass(d).wait_send()
-        s_copy(d).wait_send()
-        zr_copy(d).wait_send()
-        zb_copy(d).wait_send()
-        b_copy(d).wait_send()
         tp_copy(d).wait_send()
         xa_copy(d).wait_send()
-    v_own.wait_send()
-    for step in moves:
-        for move in step:
-            ring(*move).wait_send()
-            ring_pass(*move).wait_send()
-    for item in (swap_a, swap_s, swap_u, swap_z, swap_m, swap_t, swap_b, swap_x):
+    for item in (swap_t, swap_b, swap_x):
         item.wait_send()
-    for d in range(1, NX):
-        y_copy(d).wait_send()
-        ar_copy(ar_a, x, d, xpeer(d)).wait_send()
-        ar_copy(ar_b, leaf, 4 + d, ypeer(d)).wait_send()
-        ar_copy(ar_c, leaf, 8 + d, ypeer(d)).wait_send()
-        ar_copy(ar_d, x, 12 + d, xpeer(d)).wait_send()
-
-    @pl.when(x < NX - 1)
-    def _():
-        hop_f.wait_send()
 
     @pl.when(x > 0)
     def _():

time: 102 us -> 100 us (0.980)
  Pallas kernels: 96.5 us -> 94.7 us
    pallas_call x1, Pallas kernels: 96.5 us -> 94.7 us  [shards(): pl.pallas_call(kernel, out_shape=(jax.ShapeDtypeStruct((LOC + 1, W, W), F...]
where the time goes in v3:
time: 100 us
  Pallas kernels  94.7 us (95%)
  local copies, waits for them, and re-layouts  4.28 us (4%)
  between operations  1.3 us (1%)
    pallas_call x1, Pallas kernels, shards(): pl.pallas_call(kernel, out_shape=(jax.ShapeDtypeStruct((LOC + 1, W, W), F...  94.7 us
    unnamed x4, local copies, waits for them, and re-layouts  4.28 us

profile of v3, /device:TPU:1, one launch (start us, length us, event | category | flops | bytes accessed | tf_op | source)
XLA Modules:
  0.0 100.3 jit_solution(6757541063245487869)
XLA Ops:
  1.3 94.7 %shard_map.131 = (f32[9,256,256]{2,1,0:T(8,128)}, f32[4,256,256]{2,1,0:T(8,128)}) custom-call(s32[2,8]{1,0:T(2,128)} %bitcast.20, s32[1]{0:T(128)} %bitcast.12.target, f32[9,256,256]{2,1,0:T(8,128)} %bitcast.14, f32[9,256,256]{2,1,0:T(8,128)} %bitcast.15, f32[8,128,256]{2,1,0:T(8,128)} %bitcast.16, f32[256,256]{1,0:T(8,128)} %bitcast.17, ...), custom_call_target="tpu_custom_call" | custom-call | tf_op jit(solution)/shard_map/pallas_call | solution.py:693
  96.0 0.0 copy-start
  96.0 3.3 %copy.17 = f32[1,1,9,256,256]{4,3,2,1,0:T(8,128)} copy(f32[1,1,9,256,256]{4,3,2,1,0:T(8,128)} %bitcast.13) | data formatting | bytes 4718592
  99.3 0.0 copy-done
  99.3 1.0 copy.18
Async XLA Ops:
  96.0 3.3 %copy-start = (f32[4,256,256]{2,1,0:T(8,128)S(1)}, f32[4,256,256]{2,1,0:T(8,128)}, u32[]{:S(2)}) copy-start(f32[4,256,256]{2,1,0:T(8,128)} %get-tuple-element.9) | copy-start | bytes 3145732

commit v4 on v3

--- a/solution.py
+++ b/solution.py
@@ -342,43 +342,42 @@
 
     lax.fori_loop(1, NZ, prefix, 0)
 
+    @pl.when(x >= 2)
+    def _():
+        by_four(square)
+
+    whole = (fh[NZ - 1], fl[NZ - 1])
+    hop_f = copy(xout_f, xin_f, xf_s.at[0], xf_r.at[0], at(lax.rem(x + 1, NX), z, q))
+
+    @pl.when(x == 0)
+    def _():
+        xin_f[...] = jnp.zeros((Q, W), F32)
+        xout_f[...] = z0[NZ - 1]
+
+    @pl.when(x > 0)
+    def _():
+        hop_f.wait_recv()
+        xout_f[...] = z0[NZ - 1] + nn(xin_f[...], whole)
+
+    @pl.when(x < NX - 1)
+    def _():
+        hop_f.start()
+
+    for d in range(1, NY):
+        copy(uph.at[0], ybuf.at[yfrom(d)], y_s.at[d], y_r.at[d], ypeer(d)).wait_recv()
+    uy[...] = (ybuf[0] + ybuf[1]) + (ybuf[2] + ybuf[3])
+
     def zr_copy(d):
         to = lax.rem(z + d, NZ)
         return copy(uy.at[rows_of(to)], zred.at[z], zr_s.at[d], zr_r.at[d], zpeer(d))
 
-    def aside():
-        for d in range(1, NY):
-            copy(uph.at[0], ybuf.at[yfrom(d)], y_s.at[d], y_r.at[d], ypeer(d)).wait_recv()
-        uy[...] = (ybuf[0] + ybuf[1]) + (ybuf[2] + ybuf[3])
-        for d in order:
-            zr_copy(d).start()
-        zred[z] = uy[rows_of(z)]
+    for d in order:
+        zr_copy(d).start()
+    zred[z] = uy[rows_of(z)]
+
+    @pl.when(x < 2)
+    def _():
         by_four(square)
-
-    @pl.when(x >= 2)
-    def _():
-        aside()
-
-    whole = (fh[NZ - 1], fl[NZ - 1])
-    hop_f = copy(xout_f, xin_f, xf_s.at[0], xf_r.at[0], at(lax.rem(x + 1, NX), z, q))
-
-    @pl.when(x == 0)
-    def _():
-        xin_f[...] = jnp.zeros((Q, W), F32)
-        xout_f[...] = z0[NZ - 1]
-
-    @pl.when(x > 0)
-    def _():
-        hop_f.wait_recv()
-        xout_f[...] = z0[NZ - 1] + nn(xin_f[...], whole)
-
-    @pl.when(x < NX - 1)
-    def _():
-        hop_f.start()
-
-    @pl.when(x < 2)
-    def _():
-        aside()
 
     entering = split(xin_f[...])
     zsend[0] = xin_f[...]

time: 100 us -> 98.8 us (0.988)
  Pallas kernels: 94.7 us -> 93.2 us
    pallas_call x1, Pallas kernels: 94.7 us -> 93.2 us  [shards(): pl.pallas_call(kernel, out_shape=(jax.ShapeDtypeStruct((LOC + 1, W, W), F...]
where the time goes in v4:
time: 98.8 us; the launch traced here: 98.7 us
  Pallas kernels  93.2 us (94%)
  local copies, waits for them, and re-layouts  4.28 us (4%)
  between operations  1.3 us (1%)
    pallas_call x1, Pallas kernels, shards(): pl.pallas_call(kernel, out_shape=(jax.ShapeDtypeStruct((LOC + 1, W, W), F...  93.2 us
    unnamed x4, local copies, waits for them, and re-layouts  4.28 us

profile of v4, /device:TPU:1, one launch (start us, length us, event | category | flops | bytes accessed | tf_op | source)
XLA Modules:
  0.0 98.7 jit_solution(13384912990495666306)
XLA Ops:
  1.3 93.2 %shard_map.131 = (f32[9,256,256]{2,1,0:T(8,128)}, f32[4,256,256]{2,1,0:T(8,128)}) custom-call(s32[2,8]{1,0:T(2,128)} %bitcast.20, s32[1]{0:T(128)} %bitcast.12.target, f32[9,256,256]{2,1,0:T(8,128)} %bitcast.14, f32[9,256,256]{2,1,0:T(8,128)} %bitcast.15, f32[8,128,256]{2,1,0:T(8,128)} %bitcast.16, f32[256,256]{1,0:T(8,128)} %bitcast.17, ...), custom_call_target="tpu_custom_call" | custom-call | tf_op jit(solution)/shard_map/pallas_call | solution.py:692
  94.4 0.0 copy-start
  94.5 3.3 %copy.17 = f32[1,1,9,256,256]{4,3,2,1,0:T(8,128)} copy(f32[1,1,9,256,256]{4,3,2,1,0:T(8,128)} %bitcast.13) | data formatting | bytes 4718592
  97.8 0.0 copy-done
  97.8 1.0 copy.18
Async XLA Ops:
  94.4 3.3 %copy-start = (f32[4,256,256]{2,1,0:T(8,128)S(1)}, f32[4,256,256]{2,1,0:T(8,128)}, u32[]{:S(2)}) copy-start(f32[4,256,256]{2,1,0:T(8,128)} %get-tuple-element.9) | copy-start | bytes 3145732

commit v5 on v4

--- a/solution.py
+++ b/solution.py
@@ -217,6 +217,7 @@
         return copy(vbuf.at[z, q], vbuf.at[z, q], v_s.at[d], v_r.at[d], zpeer(d))
 
     order = (1, 7, 2, 6, 3, 5, 4)
+    direct = (5, 3, 2, 6, 1, 7)
     v_own = copy(vbuf.at[z, q], vbuf.at[z, q], vo_s.at[0], vo_r.at[0], sibling)
     v_own.start()
     some_maps(0)
@@ -248,7 +249,7 @@
         s_copy(d).start()
     sbuf[z] = schip[rows_of(z)]
 
-    for d in order:
+    for d in direct:
         v_copy(d).start()
 
     ring_step(4)
@@ -342,6 +343,11 @@
 
     lax.fori_loop(1, NZ, prefix, 0)
 
+    v_come(5).wait_recv()
+    third = vbuf.at[zfrom(5), q]
+    copy(third, third, v_s.at[4], v_r.at[4], zpeer(7)).start()
+    v_pass(5).start()
+
     @pl.when(x >= 2)
     def _():
         by_four(square)
@@ -396,7 +402,7 @@
         zb_copy(d).start()
     zback[rows_of(z)] = zsend[z]
 
-    for d in order:
+    for d in (3, 2, 6, 1, 7, 4):
         v_come(d).wait_recv()
         v_pass(d).start()
     v_own_come = copy(vbuf.at[z, 1 - q], vbuf.at[z, 1 - q], vo_s.at[0], vo_r.at[0], sibling)
@@ -504,7 +510,7 @@
     def tp_copy(d):
         return copy(topx, topt.at[:, mine_rows], tp_s.at[d], tp_r.at[d], zpeer(d))
 
-    for d in order:
+    for d in direct:
         tp_copy(d).start()
     topt[:, mine_rows] = topx[...]
 
@@ -527,6 +533,13 @@
     swap_b = swap(mb_s, mb_r, 4)
 
     def with_top():
+        def top_come(d):
+            place = pl.ds(pl.multiple_of(q * H + zfrom(d) * Q, Q), Q)
+            return copy(topx, topt.at[:, place], tp_s.at[d], tp_r.at[d], zpeer(d))
+
+        top_come(5).wait_recv()
+        third = topt.at[:, pl.ds(pl.multiple_of(q * H + zfrom(5) * Q, Q), Q)]
+        copy(third, third, tp_s.at[4], tp_r.at[4], zpeer(7)).start()
         for d in order:
             v_copy(d).wait_send()
             v_pass(d).wait_send()
@@ -552,9 +565,8 @@
         def _():
             hop_f.wait_send()
 
-        for d in order:
-            place = pl.ds(pl.multiple_of(q * H + zfrom(d) * Q, Q), Q)
-            copy(topx, topt.at[:, place], tp_s.at[d], tp_r.at[d], zpeer(d)).wait_recv()
+        for d in (3, 2, 6, 1, 7, 4):
+            top_come(d).wait_recv()
         swap_t.start()
         copy(topt.at[:, other], topt.at[:, other], up_s.at[1], up_r.at[1], sibling).wait_recv()
         pick, pick_chain = 0.0, 0.0

time: 98.8 us -> 99.4 us (level)
  no operation moved by 1% of the time
where the time goes in v5:
time: 99.4 us; the launch traced here: 99.3 us
  Pallas kernels  93.7 us (94%)
  local copies, waits for them, and re-layouts  4.28 us (4%)
  between operations  1.3 us (1%)
    pallas_call x1, Pallas kernels, shards(): pl.pallas_call(kernel, out_shape=(jax.ShapeDtypeStruct((LOC + 1, W, W), F...  93.7 us
    unnamed x4, local copies, waits for them, and re-layouts  4.28 us

profile of v5, /device:TPU:1, one launch (start us, length us, event | category | flops | bytes accessed | tf_op | source)
XLA Modules:
  0.0 99.3 jit_solution(4637818205428764609)
XLA Ops:
  1.3 93.7 %shard_map.131 = (f32[9,256,256]{2,1,0:T(8,128)}, f32[4,256,256]{2,1,0:T(8,128)}) custom-call(s32[2,8]{1,0:T(2,128)} %bitcast.20, s32[1]{0:T(128)} %bitcast.12.target, f32[9,256,256]{2,1,0:T(8,128)} %bitcast.14, f32[9,256,256]{2,1,0:T(8,128)} %bitcast.15, f32[8,128,256]{2,1,0:T(8,128)} %bitcast.16, f32[256,256]{1,0:T(8,128)} %bitcast.17, ...), custom_call_target="tpu_custom_call" | custom-call | tf_op jit(solution)/shard_map/pallas_call | solution.py:704
  95.0 0.0 copy-start
  95.0 3.3 %copy.17 = f32[1,1,9,256,256]{4,3,2,1,0:T(8,128)} copy(f32[1,1,9,256,256]{4,3,2,1,0:T(8,128)} %bitcast.13) | data formatting | bytes 4718592
  98.3 0.0 copy-done
  98.3 1.0 copy.18
Async XLA Ops:
  95.0 3.3 %copy-start = (f32[4,256,256]{2,1,0:T(8,128)S(1)}, f32[4,256,256]{2,1,0:T(8,128)}, u32[]{:S(2)}) copy-start(f32[4,256,256]{2,1,0:T(8,128)} %get-tuple-element.9) | copy-start | bytes 3145732
